TPU v7x, 512 devices: a whole 4x4x16 slice. The times are simulated.
512 devices in a mesh: grp: 16 (over y, x), tile: 32 (over z, core).
Axes of the slice: x: 4, y: 4, z: 16, core: 2. Of those that a mesh axis runs over, the one named last changes fastest.
Arguments:
- latent: bfloat16 [8, 64, 64, 512], P(None, 'grp', 'tile'), may hold values from -36 to 36
- coarse_filters: bfloat16 [3, 3, 3, 512, 512], P(None, None, None, None, 'grp'), may hold values from -0.0546875 to 0.0546875
- mid_filters: bfloat16 [3, 3, 3, 256, 256], P(None, None, None, None, 'tile'), may hold values from -0.078125 to 0.078125
- fine_filters: bfloat16 [3, 3, 3, 128, 128], replicated, may hold values from -0.109375 to 0.109375
- coarse_proj: bfloat16 [512, 256], replicated, may hold values from -0.25 to 0.25
- mid_proj: bfloat16 [256, 128], replicated, may hold values from -0.375 to 0.375
Outputs:
- frames_out: bfloat16 [8, 256, 256, 128], P(None, 'grp', 'tile')
All inputs are finite; a program needn't handle non-finite values.
Results may differ from a plain program's by a relative error of at most 0.018.
Values may be sent and summed in bfloat16 or wider, within the bound.
A program may use at most 128 MiB of HBM per device.

v0:
```python
import jax
import jax.numpy as jnp
from jax import lax
from jax.sharding import PartitionSpec as P


def with_halo(shard, sides, width):
    for axis, dim in sides:
        size, length = (lax.axis_size(axis), shard.shape[dim])
        up = [(i, (i + 1) % size) for i in range(size - 1)]
        down = [(j, i) for i, j in up]
        last = lax.slice_in_dim(shard, length - width, length, axis=dim)
        initial = lax.slice_in_dim(shard, 0, width, axis=dim)
        before = lax.ppermute(last, axis, up)
        after = lax.ppermute(initial, axis, down)
        shard = jnp.concatenate([before, shard, after], axis=dim)
    return shard


def activate(values):
    widened = values.astype(jnp.float32)
    scaled = widened * lax.rsqrt(jnp.mean(widened * widened, axis=-1, keepdims=True) + 1e-06)
    return jax.nn.silu(scaled).astype(jnp.bfloat16)


def double_size(values):
    return jnp.repeat(jnp.repeat(values, 2, axis=1), 2, axis=2)


def time_padded(values):
    return jnp.pad(values, ((2, 0), (0, 0), (0, 0), (0, 0)))


def stencil_columns(extended):
    padded = time_padded(extended)
    height = extended.shape[1] - 2
    breadth = extended.shape[2] - 2
    return jnp.concatenate(
        [
            padded[:, row_step : row_step + height, col_step : col_step + breadth, :]
            for row_step in range(3)
            for col_step in range(3)
        ],
        axis=-1,
    )


def apply_columns(columns, filters):
    frames = columns.shape[0] - 2
    folded = filters.reshape(3, 9 * filters.shape[3], filters.shape[4])
    total = jnp.dot(columns[0:frames], folded[0], preferred_element_type=jnp.float32)
    for frame_step in (1, 2):
        total = total + jnp.dot(
            columns[frame_step : frame_step + frames],
            folded[frame_step],
            preferred_element_type=jnp.float32,
        )
    return total


def coarse_conv(extended, filters):
    padded = time_padded(extended)
    frames = extended.shape[0]
    height = extended.shape[1] - 2
    breadth = extended.shape[2] - 2
    inputs = filters.shape[3]
    outputs = filters.shape[4]
    total = jnp.zeros((frames, height, breadth, outputs), jnp.float32)
    for frame_step in range(3):
        spread = jnp.transpose(filters[frame_step], (2, 0, 1, 3)).reshape(inputs, 9 * outputs)
        products = jnp.dot(
            padded[frame_step : frame_step + frames], spread, preferred_element_type=jnp.float32
        )
        for row_step in range(3):
            for col_step in range(3):
                lane = 3 * row_step + col_step
                total = (
                    total
                    + products[
                        :,
                        row_step : row_step + height,
                        col_step : col_step + breadth,
                        lane * outputs : (lane + 1) * outputs,
                    ]
                )
    return total


def middle_conv(extended, mid_filters):
    columns = stencil_columns(extended)
    return apply_columns(columns, lax.all_gather(mid_filters, "tile", axis=4, tiled=True))


def body(latent, coarse_filters, mid_filters, fine_filters, coarse_proj, mid_proj):
    first_act = activate(latent)
    whole = lax.all_gather(first_act, "grp", axis=1, tiled=True)
    widened = with_halo(whole, (("tile", 2),), 1)
    padded = jnp.pad(widened, ((0, 0), (1, 1), (0, 0), (0, 0)))
    filtered = coarse_conv(padded, coarse_filters).astype(jnp.bfloat16)
    returned = lax.all_to_all(filtered, "grp", split_axis=1, concat_axis=3, tiled=True)
    level_zero = (latent.astype(jnp.float32) + returned.astype(jnp.float32)).astype(jnp.bfloat16)
    reduced = jnp.dot(level_zero, coarse_proj, preferred_element_type=jnp.float32).astype(
        jnp.bfloat16
    )
    mid_act = double_size(activate(reduced))
    mid_ext = with_halo(mid_act, (("grp", 1), ("tile", 2)), 1)
    mid_terms = middle_conv(mid_ext, mid_filters)
    mid_out = (double_size(reduced).astype(jnp.float32) + mid_terms).astype(jnp.bfloat16)
    fine_low = jnp.dot(mid_out, mid_proj, preferred_element_type=jnp.float32).astype(jnp.bfloat16)
    fine_in = double_size(fine_low)
    fine_act = double_size(activate(fine_low))
    fine_ext = with_halo(fine_act, (("grp", 1), ("tile", 2)), 1)
    fine_terms = apply_columns(stencil_columns(fine_ext), fine_filters)
    return (fine_in.astype(jnp.float32) + fine_terms).astype(jnp.bfloat16)


def solution(mesh):
    in_specs = (
        P(None, "grp", "tile", None),
        P(None, None, None, None, "grp"),
        P(None, None, None, None, "tile"),
        P(),
        P(),
        P(),
    )
    out_specs = P(None, "grp", "tile", None)
    return jax.shard_map(body, mesh=mesh, in_specs=in_specs, out_specs=out_specs, check_vma=False)
```

profile of v0, /device:TPU:7, one launch (start us, length us, event | category | flops | bytes accessed | tf_op | source)
XLA Modules:
  0.0 200.4 jit_solution(11646952750403236550)
XLA Ops:
  7.6 1.6 fusion.33
  10.0 61.1 %all-gather.3.cloned.1.call-done = bf16[8,64,2,512]{3,0,2,1:T(8,128)(2,1)} async-done(((bf16[8,4,2,512]{3,0,2,1:T(8,128)(2,1)}), bf16[8,64,2,512]{3,0,2,1:T(8,128)(2,1)}) %all-gather.3.cloned.1.call-update) | async-done | bytes 1048592 | tf_op jit(solution)/shard_map/all_gather | solution.py:96
  71.1 1.8 copy.25
  73.0 5.1 %collective-permute-start = (bf16[8,64,1,512]{3,1,2,0:T(8,128)(2,1)S(1)}, bf16[8,64,1,512]{3,1,2,0:T(8,128)(2,1)S(1)}, u32[]{:S(2)}, u32[]{:S(2)}) collective-permute-start(bf16[8,64,1,512]{3,1,2,0:T(8,128)(2,1)S(1)} %get-tuple-element.8), channel_id=1, source_target_pairs={{0,1},{1,2},{2,3},{3,4},{4,5},{5,6},{6,7},{7,8},{8,9},{9,10},{10,1... | collective-permute-start | bytes 1572872 | tf_op jit(solution)/shard_map/ppermute | solution.py:14
  78.0 1.9 collective-permute-start.1
  80.0 4.1 %collective-permute-done = bf16[8,64,1,512]{3,1,2,0:T(8,128)(2,1)S(1)} collective-permute-done((bf16[8,64,1,512]{3,1,2,0:T(8,128)(2,1)S(1)}, bf16[8,64,1,512]{3,1,2,0:T(8,128)(2,1)S(1)}, u32[]{:S(2)}, u32[]{:S(2)}) %collective-permute-start) | collective-permute-done | bytes 524320 | tf_op jit(solution)/shard_map/ppermute | solution.py:14
  84.1 4.4 %collective-permute-done.1 = bf16[8,64,1,512]{3,1,2,0:T(8,128)(2,1)S(1)} collective-permute-done((bf16[8,64,1,512]{3,1,2,0:T(8,128)(2,1)S(1)}, bf16[8,64,1,512]{3,1,2,0:T(8,128)(2,1)S(1)}, u32[]{:S(2)}, u32[]{:S(2)}) %collective-permute-start.1) | collective-permute-done | bytes 524320 | tf_op jit(solution)/shard_map/ppermute | solution.py:15
  89.6 1.4 fusion.47
  91.0 1.4 fusion.50
  92.5 1.4 fusion.51
  93.9 2.5 %fusion.24 = bf16[8,64,2,32]{3,1,2,0:T(8,128)(2,1)S(1)} fusion(f32[8,66,4,288]{3,1,2,0:T(8,128)S(1)} %fusion.47, f32[8,66,4,288]{3,1,2,0:T(8,128)S(1)} %fusion.51, f32[8,66,4,288]{3,1,2,0:T(8,128)S(1)} %fusion.50), kind=kLoop, calls=%fused_computation.35 | loop fusion | flops 884736 | bytes 3604480 | tf_op jit(solution)/shard_map/convert_element_type | solution.py:99
  97.0 9.8 %all_to_all.4 = bf16[16,2,1024]{2,1,0:T(2,128)(2,1)S(1)} all-to-all(bf16[16,2,1024]{2,1,0:T(2,128)(2,1)S(1)} %reshape.91), channel_id=1, replica_groups=mesh['grp'=16,'tile'=32] {'grp'}, dimensions={0} | all-to-all | bytes 131072 | tf_op jit(solution)/shard_map/all_to_all | solution.py:100
  108.0 3.7 %collective-permute-start.2 = (bf16[8,1,4,256]{3,2,1,0:T(4,128)(2,1)S(1)}, bf16[8,1,4,256]{3,2,1,0:T(4,128)(2,1)S(1)}, u32[]{:S(2)}, u32[]{:S(2)}) collective-permute-start(bf16[8,1,4,256]{3,2,1,0:T(4,128)(2,1)S(1)} %get-tuple-element.23), channel_id=1, source_target_pairs={{0,32},{32,64},{64,96},{96,128},{128,160},{160,192},{192,224},{224... | collective-permute-start | bytes 49160 | tf_op jit(solution)/shard_map/ppermute | solution.py:14
  111.7 1.9 collective-permute-start.3
  113.7 4.6 %collective-permute-done.3 = bf16[8,1,4,256]{3,2,1,0:T(4,128)(2,1)S(1)} collective-permute-done((bf16[8,1,4,256]{3,2,1,0:T(4,128)(2,1)S(1)}, bf16[8,1,4,256]{3,2,1,0:T(4,128)(2,1)S(1)}, u32[]{:S(2)}, u32[]{:S(2)}) %collective-permute-start.3) | collective-permute-done | bytes 16416 | tf_op jit(solution)/shard_map/ppermute | solution.py:15
  118.4 4.6 %collective-permute-start.4 = (bf16[8,10,1,256]{3,2,1,0:T(2,128)(2,1)S(1)}, bf16[8,10,1,256]{3,2,1,0:T(2,128)(2,1)S(1)}, u32[]{:S(2)}, u32[]{:S(2)}) collective-permute-start(bf16[8,10,1,256]{3,2,1,0:T(2,128)(2,1)S(1)} %get-tuple-element.20), channel_id=1, source_target_pairs={{0,1},{1,2},{2,3},{3,4},{4,5},{5,6},{6,7},{7,8},{8,9},{9,10},{10,1... | collective-permute-start | bytes 122888 | tf_op jit(solution)/shard_map/ppermute | solution.py:14
  123.1 2.1 %collective-permute-start.5 = (bf16[8,10,1,256]{3,2,1,0:T(2,128)(2,1)S(1)}, bf16[8,10,1,256]{3,2,1,0:T(2,128)(2,1)S(1)}, u32[]{:S(2)}, u32[]{:S(2)}) collective-permute-start(bf16[8,10,1,256]{3,2,1,0:T(2,128)(2,1)S(1)} %get-tuple-element.21), channel_id=1, source_target_pairs={{1,0},{2,1},{3,2},{4,3},{5,4},{6,5},{7,6},{8,7},{9,8},{10,9},{11,1... | collective-permute-start | bytes 122888 | tf_op jit(solution)/shard_map/ppermute | solution.py:15
  125.6 3.7 %collective-permute-done.5 = bf16[8,10,1,256]{3,2,1,0:T(2,128)(2,1)S(1)} collective-permute-done((bf16[8,10,1,256]{3,2,1,0:T(2,128)(2,1)S(1)}, bf16[8,10,1,256]{3,2,1,0:T(2,128)(2,1)S(1)}, u32[]{:S(2)}, u32[]{:S(2)}) %collective-permute-start.5) | collective-permute-done | bytes 40992 | tf_op jit(solution)/shard_map/ppermute | solution.py:15
  136.8 16.2 %all-gather.5.cloned.1.call-done = bf16[3,3,3,256,256]{3,4,2,1,0:T(8,128)(2,1)} async-done(((bf16[3,3,3,256,8]{3,4,2,1,0:T(8,128)(2,1)}), bf16[3,3,3,256,256]{3,4,2,1,0:T(8,128)(2,1)}) %all-gather.5.cloned.1.call-update) | async-done | bytes 3538960 | tf_op jit(solution)/shard_map/all_gather | solution.py:91
  153.0 3.3 %fusion.40 = (bf16[1,3,3,256,256]{3,4,2,1,0:T(8,128)(2,1)S(1)}, bf16[1,3,3,256,256]{3,4,2,1,0:T(8,128)(2,1)S(1)}, bf16[1,3,3,256,256]{3,4,2,1,0:T(8,128)(2,1)}) fusion(bf16[3,3,3,256,256]{3,4,2,1,0:T(8,128)(2,1)} %all-gather.5.cloned.1.call-done), kind=kLoop, calls=%fused_computation.110 | loop fusion | bytes 7077888 | tf_op jit(solution)/shard_map/slice | solution.py:55
  156.3 2.4 %copy.49 = bf16[1,3,3,256,256]{4,3,2,1,0:T(8,128)(2,1)} copy(bf16[1,3,3,256,256]{3,4,2,1,0:T(8,128)(2,1)} %get-tuple-element.7) | data formatting | bytes 2359296
  158.7 1.6 copy.50
  161.0 2.4 %fusion.48 = f32[8,8,4,256]{3,2,1,0:T(4,128)S(1)} fusion(bf16[10,8,4,2304]{3,2,1,0:T(4,128)(2,1)} %slice_dynamic-update-slice_fusion.9, bf16[2304,256,1,1]{1,0,3,2:T(8,128)(2,1)} %bitcast.115), kind=kOutput, calls=%fused_computation.119 | convolution fusion | flops 301989888 | bytes 2916352 | tf_op jit(solution)/shard_map/dot_general | solution.py:51
  163.4 2.0 convolution_add_fusion.3
  165.4 2.1 %fusion.14 = bf16[8,8,4,256]{3,2,1,0:T(4,128)(2,1)S(1)} fusion(f32[8,8,4,256]{3,2,1,0:T(4,128)S(1)} %convert_element_type.86, f32[8,8,4,256]{3,2,1,0:T(4,128)S(1)} %convolution_add_fusion.3, bf16[10,8,4,2304]{3,2,1,0:T(4,128)(2,1)} %slice_dynamic-update-slice_fusion.9, bf16[2304,256,1,1]{1,0,3,2:T(8,128)(2,1)S(1)} %bitcast.114), kind=kOutput, calls=%fused_computation.21 | convolution fusion | flops 302186496 | bytes 3309568 | tf_op jit(solution)/shard_map/dot_general | solution.py:53
  168.2 2.7 %collective-permute-start.6 = (bf16[8,1,8,128]{3,2,1,0:T(8,128)(2,1)S(1)}, bf16[8,1,8,128]{3,2,1,0:T(8,128)(2,1)S(1)}, u32[]{:S(2)}, u32[]{:S(2)}) collective-permute-start(bf16[8,1,8,128]{3,2,1,0:T(8,128)(2,1)S(1)} %get-tuple-element.18), channel_id=1, source_target_pairs={{0,32},{32,64},{64,96},{96,128},{128,160},{160,192},{192,224},{224... | collective-permute-start | bytes 49160 | tf_op jit(solution)/shard_map/ppermute | solution.py:14
  170.9 2.6 %collective-permute-start.7 = (bf16[8,1,8,128]{3,2,1,0:T(8,128)(2,1)S(1)}, bf16[8,1,8,128]{3,2,1,0:T(8,128)(2,1)S(1)}, u32[]{:S(2)}, u32[]{:S(2)}) collective-permute-start(bf16[8,1,8,128]{3,2,1,0:T(8,128)(2,1)S(1)} %get-tuple-element.19), channel_id=1, source_target_pairs={{32,0},{64,32},{96,64},{128,96},{160,128},{192,160},{224,192},{256... | collective-permute-start | bytes 49160 | tf_op jit(solution)/shard_map/ppermute | solution.py:15
  173.5 4.0 %collective-permute-done.7 = bf16[8,1,8,128]{3,2,1,0:T(8,128)(2,1)S(1)} collective-permute-done((bf16[8,1,8,128]{3,2,1,0:T(8,128)(2,1)S(1)}, bf16[8,1,8,128]{3,2,1,0:T(8,128)(2,1)S(1)}, u32[]{:S(2)}, u32[]{:S(2)}) %collective-permute-start.7) | collective-permute-done | bytes 16416 | tf_op jit(solution)/shard_map/ppermute | solution.py:15
  177.6 5.2 %collective-permute-start.8 = (bf16[8,18,1,128]{3,2,1,0:T(2,128)(2,1)S(1)}, bf16[8,18,1,128]{3,2,1,0:T(2,128)(2,1)S(1)}, u32[]{:S(2)}, u32[]{:S(2)}) collective-permute-start(bf16[8,18,1,128]{3,2,1,0:T(2,128)(2,1)S(1)} %get-tuple-element.16), channel_id=1, source_target_pairs={{0,1},{1,2},{2,3},{3,4},{4,5},{5,6},{6,7},{7,8},{8,9},{9,10},{10,1... | collective-permute-start | bytes 110600 | tf_op jit(solution)/shard_map/ppermute | solution.py:14
  182.9 1.9 collective-permute-start.9
  184.9 3.6 %collective-permute-done.9 = bf16[8,18,1,128]{3,2,1,0:T(2,128)(2,1)S(1)} collective-permute-done((bf16[8,18,1,128]{3,2,1,0:T(2,128)(2,1)S(1)}, bf16[8,18,1,128]{3,2,1,0:T(2,128)(2,1)S(1)}, u32[]{:S(2)}, u32[]{:S(2)}) %collective-permute-start.9) | collective-permute-done | bytes 36896 | tf_op jit(solution)/shard_map/ppermute | solution.py:15
  192.0 1.5 fusion.12
  (81 shorter events, 17.8 us)
Async XLA Ops:
  6.5 100.8 %copy-start = (bf16[512,256]{1,0:T(8,128)(2,1)S(1)}, bf16[512,256]{1,0:T(8,128)(2,1)}, u32[]{:S(2)}) copy-start(bf16[512,256]{1,0:T(8,128)(2,1)} %param.10) | copy-start | bytes 786436
  6.5 73.4 %copy-start.2 = (bf16[3,3,3,512,32]{3,4,2,1,0:T(8,128)(2,1)S(1)}, bf16[3,3,3,512,32]{3,4,2,1,0:T(8,128)(2,1)}, u32[]{:S(2)}) copy-start(bf16[3,3,3,512,32]{3,4,2,1,0:T(8,128)(2,1)} %param.7) | copy-start | bytes 2654212
  6.5 64.5 %all-gather.3.cloned.1.call-start = ((), (), s32[]{:S(2)}) async-start(), calls=%async_computation.1 | async-start | bytes 1114112 | tf_op jit(solution)/shard_map/all_gather | solution.py:96
  9.2 143.8 %all-gather.5.cloned.1.call-start = ((), (), s32[]{:S(2)}) async-start(), calls=%async_computation.2 | async-start | bytes 3649536 | tf_op jit(solution)/shard_map/all_gather | solution.py:91
  73.0 11.2 %collective-permute-start = (bf16[8,64,1,512]{3,1,2,0:T(8,128)(2,1)S(1)}, bf16[8,64,1,512]{3,1,2,0:T(8,128)(2,1)S(1)}, u32[]{:S(2)}, u32[]{:S(2)}) collective-permute-start(bf16[8,64,1,512]{3,1,2,0:T(8,128)(2,1)S(1)} %get-tuple-element.8), channel_id=1, source_target_pairs={{0,1},{1,2},{2,3},{3,4},{4,5},{5,6},{6,7},{7,8},{8,9},{9,10},{10,1... | collective-permute-start | bytes 1572872 | tf_op jit(solution)/shard_map/ppermute | solution.py:14
  78.0 10.5 %collective-permute-start.1 = (bf16[8,64,1,512]{3,1,2,0:T(8,128)(2,1)S(1)}, bf16[8,64,1,512]{3,1,2,0:T(8,128)(2,1)S(1)}, u32[]{:S(2)}, u32[]{:S(2)}) collective-permute-start(bf16[8,64,1,512]{3,1,2,0:T(8,128)(2,1)S(1)} %get-tuple-element.9), channel_id=1, source_target_pairs={{1,0},{2,1},{3,2},{4,3},{5,4},{6,5},{7,6},{8,7},{9,8},{10,9},{11,1... | collective-permute-start | bytes 1572872 | tf_op jit(solution)/shard_map/ppermute | solution.py:15
  96.4 10.9 %copy-start.4 = (bf16[8,4,2,512]{3,2,1,0:T(2,128)(2,1)S(1)}, bf16[8,4,2,512]{3,2,1,0:T(2,128)(2,1)}, u32[]{:S(2)}) copy-start(bf16[8,4,2,512]{3,2,1,0:T(2,128)(2,1)} %param.6) | copy-start | bytes 196612
  108.0 5.6 %collective-permute-start.2 = (bf16[8,1,4,256]{3,2,1,0:T(4,128)(2,1)S(1)}, bf16[8,1,4,256]{3,2,1,0:T(4,128)(2,1)S(1)}, u32[]{:S(2)}, u32[]{:S(2)}) collective-permute-start(bf16[8,1,4,256]{3,2,1,0:T(4,128)(2,1)S(1)} %get-tuple-element.23), channel_id=1, source_target_pairs={{0,32},{32,64},{64,96},{96,128},{128,160},{160,192},{192,224},{224... | collective-permute-start | bytes 49160 | tf_op jit(solution)/shard_map/ppermute | solution.py:14
  111.7 6.6 %collective-permute-start.3 = (bf16[8,1,4,256]{3,2,1,0:T(4,128)(2,1)S(1)}, bf16[8,1,4,256]{3,2,1,0:T(4,128)(2,1)S(1)}, u32[]{:S(2)}, u32[]{:S(2)}) collective-permute-start(bf16[8,1,4,256]{3,2,1,0:T(4,128)(2,1)S(1)} %get-tuple-element.22), channel_id=1, source_target_pairs={{32,0},{64,32},{96,64},{128,96},{160,128},{192,160},{224,192},{256... | collective-permute-start | bytes 49160 | tf_op jit(solution)/shard_map/ppermute | solution.py:15
  118.4 7.2 %collective-permute-start.4 = (bf16[8,10,1,256]{3,2,1,0:T(2,128)(2,1)S(1)}, bf16[8,10,1,256]{3,2,1,0:T(2,128)(2,1)S(1)}, u32[]{:S(2)}, u32[]{:S(2)}) collective-permute-start(bf16[8,10,1,256]{3,2,1,0:T(2,128)(2,1)S(1)} %get-tuple-element.20), channel_id=1, source_target_pairs={{0,1},{1,2},{2,3},{3,4},{4,5},{5,6},{6,7},{7,8},{8,9},{9,10},{10,1... | collective-permute-start | bytes 122888 | tf_op jit(solution)/shard_map/ppermute | solution.py:14
  123.1 6.3 %collective-permute-start.5 = (bf16[8,10,1,256]{3,2,1,0:T(2,128)(2,1)S(1)}, bf16[8,10,1,256]{3,2,1,0:T(2,128)(2,1)S(1)}, u32[]{:S(2)}, u32[]{:S(2)}) collective-permute-start(bf16[8,10,1,256]{3,2,1,0:T(2,128)(2,1)S(1)} %get-tuple-element.21), channel_id=1, source_target_pairs={{1,0},{2,1},{3,2},{4,3},{5,4},{6,5},{7,6},{8,7},{9,8},{10,9},{11,1... | collective-permute-start | bytes 122888 | tf_op jit(solution)/shard_map/ppermute | solution.py:15
  161.0 2.4 %copy-start.1 = (bf16[1,3,3,256,256]{4,3,2,1,0:T(8,128)(2,1)S(1)}, bf16[1,3,3,256,256]{4,3,2,1,0:T(8,128)(2,1)}, u32[]{:S(2)}) copy-start(bf16[1,3,3,256,256]{4,3,2,1,0:T(8,128)(2,1)} %copy.50) | copy-start | bytes 3538948
  165.4 2.1 %copy-start.5 = (bf16[256,128]{1,0:T(8,128)(2,1)S(1)}, bf16[256,128]{1,0:T(8,128)(2,1)}, u32[]{:S(2)}) copy-start(bf16[256,128]{1,0:T(8,128)(2,1)} %param.11) | copy-start | bytes 196612
  165.4 19.4 %copy-start.3 = (bf16[3,3,3,128,128]{4,3,2,1,0:T(8,128)(2,1)S(1)}, bf16[3,3,3,128,128]{4,3,2,1,0:T(8,128)(2,1)}, u32[]{:S(2)}) copy-start(bf16[3,3,3,128,128]{4,3,2,1,0:T(8,128)(2,1)} %param.9) | copy-start | bytes 2654212
  168.2 5.3 %collective-permute-start.6 = (bf16[8,1,8,128]{3,2,1,0:T(8,128)(2,1)S(1)}, bf16[8,1,8,128]{3,2,1,0:T(8,128)(2,1)S(1)}, u32[]{:S(2)}, u32[]{:S(2)}) collective-permute-start(bf16[8,1,8,128]{3,2,1,0:T(8,128)(2,1)S(1)} %get-tuple-element.18), channel_id=1, source_target_pairs={{0,32},{32,64},{64,96},{96,128},{128,160},{160,192},{192,224},{224... | collective-permute-start | bytes 49160 | tf_op jit(solution)/shard_map/ppermute | solution.py:14
  170.9 6.6 %collective-permute-start.7 = (bf16[8,1,8,128]{3,2,1,0:T(8,128)(2,1)S(1)}, bf16[8,1,8,128]{3,2,1,0:T(8,128)(2,1)S(1)}, u32[]{:S(2)}, u32[]{:S(2)}) collective-permute-start(bf16[8,1,8,128]{3,2,1,0:T(8,128)(2,1)S(1)} %get-tuple-element.19), channel_id=1, source_target_pairs={{32,0},{64,32},{96,64},{128,96},{160,128},{192,160},{224,192},{256... | collective-permute-start | bytes 49160 | tf_op jit(solution)/shard_map/ppermute | solution.py:15
  177.6 7.3 %collective-permute-start.8 = (bf16[8,18,1,128]{3,2,1,0:T(2,128)(2,1)S(1)}, bf16[8,18,1,128]{3,2,1,0:T(2,128)(2,1)S(1)}, u32[]{:S(2)}, u32[]{:S(2)}) collective-permute-start(bf16[8,18,1,128]{3,2,1,0:T(2,128)(2,1)S(1)} %get-tuple-element.16), channel_id=1, source_target_pairs={{0,1},{1,2},{2,3},{3,4},{4,5},{5,6},{6,7},{7,8},{8,9},{9,10},{10,1... | collective-permute-start | bytes 110600 | tf_op jit(solution)/shard_map/ppermute | solution.py:14
  182.9 5.7 %collective-permute-start.9 = (bf16[8,18,1,128]{3,2,1,0:T(2,128)(2,1)S(1)}, bf16[8,18,1,128]{3,2,1,0:T(2,128)(2,1)S(1)}, u32[]{:S(2)}, u32[]{:S(2)}) collective-permute-start(bf16[8,18,1,128]{3,2,1,0:T(2,128)(2,1)S(1)} %get-tuple-element.17), channel_id=1, source_target_pairs={{1,0},{2,1},{3,2},{4,3},{5,4},{6,5},{7,6},{8,7},{9,8},{10,9},{11,1... | collective-permute-start | bytes 110600 | tf_op jit(solution)/shard_map/ppermute | solution.py:15
Sparse Core Ops, SparseCore 0:
  10.4 60.6 all-gather.2
  73.1 79.7 all-gather.4
where the time goes:
time: 201 us; the launch traced here: 200 us
  waiting for transfers between devices  102 us (51%)
  starting transfers between devices  31.8 us (16%)
  local copies, waits for them, and re-layouts  20.9 us (10%)
  matrix products  14.4 us (7%)
  between operations  13.9 us (7%)
  blocking collectives  9.77 us (5%)
  other arithmetic  7.18 us (4%)
    all_gather x1, waiting for transfers between devices, body(): whole = lax.all_gather(first_act, 'grp', axis=1, tiled=True)  61.1 us
    ppermute x5, starting transfers between devices, with_halo(): before = lax.ppermute(last, axis, up)  21.3 us
    ppermute x5, waiting for transfers between devices, with_halo(): after = lax.ppermute(initial, axis, down)  20.3 us
    all_gather x1, waiting for transfers between devices, middle_conv(): lax.all_gather(mid_filters, 'tile', axis=4, tiled=True)  16.2 us
    unnamed x35, local copies, waits for them, and re-layouts  12.7 us
    ppermute x5, starting transfers between devices, with_halo(): after = lax.ppermute(initial, axis, down)  10.5 us
    all_to_all x1, blocking collectives, body(): lax.all_to_all(filtered, 'grp', split_axis=1, concat_axis=3, tiled=True)  9.77 us
    dot_general x4, matrix products, apply_columns(): jnp.dot(columns[frame_step:frame_step + frames], folded[frame_step], pref...  6.33 us
  transfers between devices with their start and end apart: 12, of which 8 were waited for; matrix products, arithmetic and copies ran while one was open for 10% of the time, Pallas kernels for 0%

commit v1 on v0

--- a/solution.py
+++ b/solution.py
@@ -93,7 +93,20 @@
 
 def body(latent, coarse_filters, mid_filters, fine_filters, coarse_proj, mid_proj):
     first_act = activate(latent)
-    whole = lax.all_gather(first_act, "grp", axis=1, tiled=True)
+    ways, here, step = (lax.axis_size("grp"), lax.axis_index("grp"), first_act.shape[1])
+    shape = [n * ways if d == 1 else n for d, n in enumerate(first_act.shape)]
+    whole = lax.dynamic_update_slice_in_dim(
+        jnp.zeros(shape, first_act.dtype), first_act, here * step, axis=1
+    )
+    going_up = going_down = first_act
+    for far in range(1, ways // 2 + 1):
+        going_up = lax.ppermute(going_up, "grp", [(d, (d + 1) % ways) for d in range(ways)])
+        whole = lax.dynamic_update_slice_in_dim(whole, going_up, (here - far) % ways * step, axis=1)
+        if 2 * far < ways:
+            going_down = lax.ppermute(going_down, "grp", [(d, (d - 1) % ways) for d in range(ways)])
+            whole = lax.dynamic_update_slice_in_dim(
+                whole, going_down, (here + far) % ways * step, axis=1
+            )
     widened = with_halo(whole, (("tile", 2),), 1)
     padded = jnp.pad(widened, ((0, 0), (1, 1), (0, 0), (0, 0)))
     filtered = coarse_conv(padded, coarse_filters).astype(jnp.bfloat16)

time: 201 us -> 195 us (0.970)
  the two profiles are of different devices: /device:TPU:7 before, /device:TPU:103 now
where the time goes in v1:
time: 195 us; the launch traced here: 194 us
  starting transfers between devices  90.2 us (46%)
  waiting for transfers between devices  29 us (15%)
  local copies, waits for them, and re-layouts  20.1 us (10%)
  blocking collectives  19.1 us (10%)
  between operations  14.6 us (7%)
  matrix products  14.4 us (7%)
  other arithmetic  6.59 us (3%)
    ppermute x8, starting transfers between devices, body(): lax.ppermute(going_up, 'grp', [(d, (d + 1) % ways) for d in range(ways)])  41.3 us
    ppermute x5, starting transfers between devices, with_halo(): before = lax.ppermute(last, axis, up)  24 us
    ppermute x5, waiting for transfers between devices, with_halo(): after = lax.ppermute(initial, axis, down)  22.5 us
    all_to_all x1, blocking collectives, body(): lax.all_to_all(filtered, 'grp', split_axis=1, concat_axis=3, tiled=True)  19.1 us
    ppermute x7, starting transfers between devices, body(): lax.ppermute(going_down, 'grp', [(d, (d - 1) % ways) for d in range(ways)])  13.7 us
    unnamed x35, local copies, waits for them, and re-layouts  12.6 us
    ppermute x5, starting transfers between devices, with_halo(): after = lax.ppermute(initial, axis, down)  11.2 us
    dot_general x4, matrix products, apply_columns(): jnp.dot(columns[frame_step:frame_step + frames], folded[frame_step], pref...  6.32 us
  transfers between devices with their start and end apart: 26, of which 7 were waited for; matrix products, arithmetic and copies ran while one was open for 10% of the time, Pallas kernels for 0%

profile of v1, /device:TPU:103, one launch (start us, length us, event | category | flops | bytes accessed | tf_op | source)
XLA Modules:
  0.0 193.9 jit_solution(14795854035309251484)
XLA Ops:
  8.9 3.3 %collective-permute-start = (bf16[8,4,2,512]{3,1,2,0:T(4,128)(2,1)S(1)}, bf16[8,4,2,512]{3,1,2,0:T(4,128)(2,1)S(1)}, u32[]{:S(2)}, u32[]{:S(2)}) collective-permute-start(bf16[8,4,2,512]{3,1,2,0:T(4,128)(2,1)S(1)} %get-tuple-element.6), channel_id=1, source_target_pairs={{0,32},{32,64},{64,96},{96,128},{128,160},{160,192},{192,224},{224... | collective-permute-start | bytes 196616 | tf_op jit(solution)/shard_map/ppermute | solution.py:103
  12.2 2.2 %collective-permute-start.1 = (bf16[8,4,2,512]{3,1,2,0:T(4,128)(2,1)S(1)}, bf16[8,4,2,512]{3,1,2,0:T(4,128)(2,1)S(1)}, u32[]{:S(2)}, u32[]{:S(2)}) collective-permute-start(bf16[8,4,2,512]{3,1,2,0:T(4,128)(2,1)S(1)} %get-tuple-element.6), channel_id=1, source_target_pairs={{0,480},{32,0},{64,32},{96,64},{128,96},{160,128},{192,160},{224,1... | collective-permute-start | bytes 196616 | tf_op jit(solution)/shard_map/ppermute | solution.py:106
  14.6 5.2 %collective-permute-start.2 = (bf16[8,4,2,512]{3,1,2,0:T(4,128)(2,1)S(1)}, bf16[8,4,2,512]{3,1,2,0:T(4,128)(2,1)S(1)}, u32[]{:S(2)}, u32[]{:S(2)}) collective-permute-start(bf16[8,4,2,512]{3,1,2,0:T(4,128)(2,1)S(1)} %collective-permute-done), channel_id=1, source_target_pairs={{0,32},{32,64},{64,96},{96,128},{128,160},{160,192},{192,224},{224... | collective-permute-start | bytes 196616 | tf_op jit(solution)/shard_map/ppermute | solution.py:103
  19.9 1.9 collective-permute-start.3
  21.9 5.5 %collective-permute-start.4 = (bf16[8,4,2,512]{3,1,2,0:T(4,128)(2,1)S(1)}, bf16[8,4,2,512]{3,1,2,0:T(4,128)(2,1)S(1)}, u32[]{:S(2)}, u32[]{:S(2)}) collective-permute-start(bf16[8,4,2,512]{3,1,2,0:T(4,128)(2,1)S(1)} %collective-permute-done.2), channel_id=1, source_target_pairs={{0,32},{32,64},{64,96},{96,128},{128,160},{160,192},{192,224},{224... | collective-permute-start | bytes 196616 | tf_op jit(solution)/shard_map/ppermute | solution.py:103
  27.4 1.9 collective-permute-start.5
  29.5 5.5 %collective-permute-start.6 = (bf16[8,4,2,512]{3,1,2,0:T(4,128)(2,1)S(1)}, bf16[8,4,2,512]{3,1,2,0:T(4,128)(2,1)S(1)}, u32[]{:S(2)}, u32[]{:S(2)}) collective-permute-start(bf16[8,4,2,512]{3,1,2,0:T(4,128)(2,1)S(1)} %collective-permute-done.4), channel_id=1, source_target_pairs={{0,32},{32,64},{64,96},{96,128},{128,160},{160,192},{192,224},{224... | collective-permute-start | bytes 196616 | tf_op jit(solution)/shard_map/ppermute | solution.py:103
  35.0 1.9 collective-permute-start.7
  37.0 5.5 %collective-permute-start.8 = (bf16[8,4,2,512]{3,1,2,0:T(4,128)(2,1)S(1)}, bf16[8,4,2,512]{3,1,2,0:T(4,128)(2,1)S(1)}, u32[]{:S(2)}, u32[]{:S(2)}) collective-permute-start(bf16[8,4,2,512]{3,1,2,0:T(4,128)(2,1)S(1)} %collective-permute-done.6), channel_id=1, source_target_pairs={{0,32},{32,64},{64,96},{96,128},{128,160},{160,192},{192,224},{224... | collective-permute-start | bytes 196616 | tf_op jit(solution)/shard_map/ppermute | solution.py:103
  44.6 5.5 %collective-permute-start.10 = (bf16[8,4,2,512]{3,1,2,0:T(4,128)(2,1)S(1)}, bf16[8,4,2,512]{3,1,2,0:T(4,128)(2,1)S(1)}, u32[]{:S(2)}, u32[]{:S(2)}) collective-permute-start(bf16[8,4,2,512]{3,1,2,0:T(4,128)(2,1)S(1)} %collective-permute-done.8), channel_id=1, source_target_pairs={{0,32},{32,64},{64,96},{96,128},{128,160},{160,192},{192,224},{224... | collective-permute-start | bytes 196616 | tf_op jit(solution)/shard_map/ppermute | solution.py:103
  52.1 5.5 %collective-permute-start.12 = (bf16[8,4,2,512]{3,1,2,0:T(4,128)(2,1)S(1)}, bf16[8,4,2,512]{3,1,2,0:T(4,128)(2,1)S(1)}, u32[]{:S(2)}, u32[]{:S(2)}) collective-permute-start(bf16[8,4,2,512]{3,1,2,0:T(4,128)(2,1)S(1)} %collective-permute-done.10), channel_id=1, source_target_pairs={{0,32},{32,64},{64,96},{96,128},{128,160},{160,192},{192,224},{224... | collective-permute-start | bytes 196616 | tf_op jit(solution)/shard_map/ppermute | solution.py:103
  59.7 5.5 %collective-permute-start.14 = (bf16[8,4,2,512]{3,1,2,0:T(4,128)(2,1)S(1)}, bf16[8,4,2,512]{3,1,2,0:T(4,128)(2,1)S(1)}, u32[]{:S(2)}, u32[]{:S(2)}) collective-permute-start(bf16[8,4,2,512]{3,1,2,0:T(4,128)(2,1)S(1)} %collective-permute-done.12), channel_id=1, source_target_pairs={{0,32},{32,64},{64,96},{96,128},{128,160},{160,192},{192,224},{224... | collective-permute-start | bytes 196616 | tf_op jit(solution)/shard_map/ppermute | solution.py:103
  66.6 11.0 %collective-permute-start.15 = (bf16[8,64,1,512]{3,1,2,0:T(8,128)(2,1)S(1)}, bf16[8,64,1,512]{3,1,2,0:T(8,128)(2,1)S(1)}, u32[]{:S(2)}, u32[]{:S(2)}) collective-permute-start(bf16[8,64,1,512]{3,1,2,0:T(8,128)(2,1)S(1)} %get-tuple-element.10), channel_id=1, source_target_pairs={{0,1},{1,2},{2,3},{3,4},{4,5},{5,6},{6,7},{7,8},{8,9},{9,10},{10,1... | collective-permute-start | bytes 1572872 | tf_op jit(solution)/shard_map/ppermute | solution.py:14
  79.6 5.3 %collective-permute-done.15 = bf16[8,64,1,512]{3,1,2,0:T(8,128)(2,1)S(1)} collective-permute-done((bf16[8,64,1,512]{3,1,2,0:T(8,128)(2,1)S(1)}, bf16[8,64,1,512]{3,1,2,0:T(8,128)(2,1)S(1)}, u32[]{:S(2)}, u32[]{:S(2)}) %collective-permute-start.15) | collective-permute-done | bytes 524320 | tf_op jit(solution)/shard_map/ppermute | solution.py:14
  84.9 5.5 %collective-permute-done.16 = bf16[8,64,1,512]{3,1,2,0:T(8,128)(2,1)S(1)} collective-permute-done((bf16[8,64,1,512]{3,1,2,0:T(8,128)(2,1)S(1)}, bf16[8,64,1,512]{3,1,2,0:T(8,128)(2,1)S(1)}, u32[]{:S(2)}, u32[]{:S(2)}) %collective-permute-start.16) | collective-permute-done | bytes 524320 | tf_op jit(solution)/shard_map/ppermute | solution.py:15
  95.7 2.5 %fusion.24 = bf16[8,64,2,32]{3,1,2,0:T(8,128)(2,1)S(1)} fusion(f32[8,66,4,288]{3,1,2,0:T(8,128)S(1)} %fusion.48, f32[8,66,4,288]{3,1,2,0:T(8,128)S(1)} %fusion.52, f32[8,66,4,288]{3,1,2,0:T(8,128)S(1)} %fusion.51), kind=kLoop, calls=%fused_computation.35 | loop fusion | flops 884736 | bytes 3604480 | tf_op jit(solution)/shard_map/convert_element_type | solution.py:112
  98.8 19.1 %all_to_all.4 = bf16[16,2,1024]{2,1,0:T(2,128)(2,1)S(1)} all-to-all(bf16[16,2,1024]{2,1,0:T(2,128)(2,1)S(1)} %reshape.91), channel_id=1, replica_groups=mesh['grp'=16,'tile'=32] {'grp'}, dimensions={0} | all-to-all | bytes 131072 | tf_op jit(solution)/shard_map/all_to_all | solution.py:113
  119.2 3.7 %collective-permute-start.17 = (bf16[8,1,4,256]{3,2,1,0:T(4,128)(2,1)S(1)}, bf16[8,1,4,256]{3,2,1,0:T(4,128)(2,1)S(1)}, u32[]{:S(2)}, u32[]{:S(2)}) collective-permute-start(bf16[8,1,4,256]{3,2,1,0:T(4,128)(2,1)S(1)} %get-tuple-element.25), channel_id=1, source_target_pairs={{0,32},{32,64},{64,96},{96,128},{128,160},{160,192},{192,224},{224... | collective-permute-start | bytes 49160 | tf_op jit(solution)/shard_map/ppermute | solution.py:14
  122.9 2.1 %collective-permute-start.18 = (bf16[8,1,4,256]{3,2,1,0:T(4,128)(2,1)S(1)}, bf16[8,1,4,256]{3,2,1,0:T(4,128)(2,1)S(1)}, u32[]{:S(2)}, u32[]{:S(2)}) collective-permute-start(bf16[8,1,4,256]{3,2,1,0:T(4,128)(2,1)S(1)} %get-tuple-element.24), channel_id=1, source_target_pairs={{32,0},{64,32},{96,64},{128,96},{160,128},{192,160},{224,192},{256... | collective-permute-start | bytes 49160 | tf_op jit(solution)/shard_map/ppermute | solution.py:15
  125.1 4.4 %collective-permute-done.18 = bf16[8,1,4,256]{3,2,1,0:T(4,128)(2,1)S(1)} collective-permute-done((bf16[8,1,4,256]{3,2,1,0:T(4,128)(2,1)S(1)}, bf16[8,1,4,256]{3,2,1,0:T(4,128)(2,1)S(1)}, u32[]{:S(2)}, u32[]{:S(2)}) %collective-permute-start.18) | collective-permute-done | bytes 16416 | tf_op jit(solution)/shard_map/ppermute | solution.py:15
  129.6 4.4 %collective-permute-start.19 = (bf16[8,10,1,256]{3,2,1,0:T(2,128)(2,1)S(1)}, bf16[8,10,1,256]{3,2,1,0:T(2,128)(2,1)S(1)}, u32[]{:S(2)}, u32[]{:S(2)}) collective-permute-start(bf16[8,10,1,256]{3,2,1,0:T(2,128)(2,1)S(1)} %get-tuple-element.22), channel_id=1, source_target_pairs={{0,1},{1,2},{2,3},{3,4},{4,5},{5,6},{6,7},{7,8},{8,9},{9,10},{10,1... | collective-permute-start | bytes 122888 | tf_op jit(solution)/shard_map/ppermute | solution.py:14
  136.4 4.6 %collective-permute-done.20 = bf16[8,10,1,256]{3,2,1,0:T(2,128)(2,1)S(1)} collective-permute-done((bf16[8,10,1,256]{3,2,1,0:T(2,128)(2,1)S(1)}, bf16[8,10,1,256]{3,2,1,0:T(2,128)(2,1)S(1)}, u32[]{:S(2)}, u32[]{:S(2)}) %collective-permute-start.20) | collective-permute-done | bytes 40992 | tf_op jit(solution)/shard_map/ppermute | solution.py:15
  148.4 3.3 %fusion.41 = (bf16[1,3,3,256,256]{3,4,2,1,0:T(8,128)(2,1)S(1)}, bf16[1,3,3,256,256]{3,4,2,1,0:T(8,128)(2,1)S(1)}, bf16[1,3,3,256,256]{3,4,2,1,0:T(8,128)(2,1)}) fusion(bf16[3,3,3,256,256]{3,4,2,1,0:T(8,128)(2,1)} %all-gather.2.cloned.1.call-done), kind=kLoop, calls=%fused_computation.127 | loop fusion | bytes 7077888 | tf_op jit(solution)/shard_map/slice | solution.py:55
  151.7 2.4 %copy.78 = bf16[1,3,3,256,256]{4,3,2,1,0:T(8,128)(2,1)} copy(bf16[1,3,3,256,256]{3,4,2,1,0:T(8,128)(2,1)} %get-tuple-element.9) | data formatting | bytes 2359296
  156.3 2.4 %fusion.49 = f32[8,8,4,256]{3,2,1,0:T(4,128)S(1)} fusion(bf16[10,8,4,2304]{3,2,1,0:T(4,128)(2,1)} %slice_dynamic-update-slice_fusion.9, bf16[2304,256,1,1]{1,0,3,2:T(8,128)(2,1)} %bitcast.115), kind=kOutput, calls=%fused_computation.136 | convolution fusion | flops 301989888 | bytes 2916352 | tf_op jit(solution)/shard_map/dot_general | solution.py:51
  158.8 2.0 %convolution_add_fusion.3 = f32[8,8,4,256]{3,2,1,0:T(4,128)S(1)} fusion(f32[8,8,4,256]{3,2,1,0:T(4,128)S(1)} %fusion.49, bf16[10,8,4,2304]{3,2,1,0:T(4,128)(2,1)} %slice_dynamic-update-slice_fusion.9, bf16[2304,256,1,1]{1,0,3,2:T(8,128)(2,1)S(1)} %bitcast.116), kind=kOutput, calls=%fused_computation.20 | convolution fusion | flops 302055424 | bytes 3178496 | tf_op jit(solution)/shard_map/dot_general | solution.py:53
  160.8 2.1 %fusion.14 = bf16[8,8,4,256]{3,2,1,0:T(4,128)(2,1)S(1)} fusion(f32[8,8,4,256]{3,2,1,0:T(4,128)S(1)} %convert_element_type.86, f32[8,8,4,256]{3,2,1,0:T(4,128)S(1)} %convolution_add_fusion.3, bf16[10,8,4,2304]{3,2,1,0:T(4,128)(2,1)} %slice_dynamic-update-slice_fusion.9, bf16[2304,256,1,1]{1,0,3,2:T(8,128)(2,1)S(1)} %bitcast.114), kind=kOutput, calls=%fused_computation.21 | convolution fusion | flops 302186496 | bytes 3309568 | tf_op jit(solution)/shard_map/dot_general | solution.py:53
  165.5 3.4 %collective-permute-start.22 = (bf16[8,1,8,128]{3,2,1,0:T(8,128)(2,1)S(1)}, bf16[8,1,8,128]{3,2,1,0:T(8,128)(2,1)S(1)}, u32[]{:S(2)}, u32[]{:S(2)}) collective-permute-start(bf16[8,1,8,128]{3,2,1,0:T(8,128)(2,1)S(1)} %get-tuple-element.21), channel_id=1, source_target_pairs={{32,0},{64,32},{96,64},{128,96},{160,128},{192,160},{224,192},{256... | collective-permute-start | bytes 49160 | tf_op jit(solution)/shard_map/ppermute | solution.py:15
  168.9 3.2 %collective-permute-done.22 = bf16[8,1,8,128]{3,2,1,0:T(8,128)(2,1)S(1)} collective-permute-done((bf16[8,1,8,128]{3,2,1,0:T(8,128)(2,1)S(1)}, bf16[8,1,8,128]{3,2,1,0:T(8,128)(2,1)S(1)}, u32[]{:S(2)}, u32[]{:S(2)}) %collective-permute-start.22) | collective-permute-done | bytes 16416 | tf_op jit(solution)/shard_map/ppermute | solution.py:15
  172.2 3.0 %collective-permute-start.23 = (bf16[8,18,1,128]{3,2,1,0:T(2,128)(2,1)S(1)}, bf16[8,18,1,128]{3,2,1,0:T(2,128)(2,1)S(1)}, u32[]{:S(2)}, u32[]{:S(2)}) collective-permute-start(bf16[8,18,1,128]{3,2,1,0:T(2,128)(2,1)S(1)} %get-tuple-element.18), channel_id=1, source_target_pairs={{0,1},{1,2},{2,3},{3,4},{4,5},{5,6},{6,7},{7,8},{8,9},{9,10},{10,1... | collective-permute-start | bytes 110600 | tf_op jit(solution)/shard_map/ppermute | solution.py:14
  175.2 1.9 collective-permute-start.24
  177.3 4.8 %collective-permute-done.24 = bf16[8,18,1,128]{3,2,1,0:T(2,128)(2,1)S(1)} collective-permute-done((bf16[8,18,1,128]{3,2,1,0:T(2,128)(2,1)S(1)}, bf16[8,18,1,128]{3,2,1,0:T(2,128)(2,1)S(1)}, u32[]{:S(2)}, u32[]{:S(2)}) %collective-permute-start.24) | collective-permute-done | bytes 36896 | tf_op jit(solution)/shard_map/ppermute | solution.py:15
  (127 shorter events, 39.1 us)
Async XLA Ops:
  6.5 112.0 %copy-start = (bf16[512,256]{1,0:T(8,128)(2,1)S(1)}, bf16[512,256]{1,0:T(8,128)(2,1)}, u32[]{:S(2)}) copy-start(bf16[512,256]{1,0:T(8,128)(2,1)} %param.10) | copy-start | bytes 786436
  6.5 141.8 %all-gather.2.cloned.1.call-start = ((), (), s32[]{:S(2)}) async-start(), calls=%async_computation.1 | async-start | bytes 3649536 | tf_op jit(solution)/shard_map/all_gather | solution.py:91
  8.9 70.7 %copy-start.2 = (bf16[3,3,3,512,32]{3,4,2,1,0:T(8,128)(2,1)S(1)}, bf16[3,3,3,512,32]{3,4,2,1,0:T(8,128)(2,1)}, u32[]{:S(2)}) copy-start(bf16[3,3,3,512,32]{3,4,2,1,0:T(8,128)(2,1)} %param.7) | copy-start | bytes 2654212
  8.9 5.7 %collective-permute-start = (bf16[8,4,2,512]{3,1,2,0:T(4,128)(2,1)S(1)}, bf16[8,4,2,512]{3,1,2,0:T(4,128)(2,1)S(1)}, u32[]{:S(2)}, u32[]{:S(2)}) collective-permute-start(bf16[8,4,2,512]{3,1,2,0:T(4,128)(2,1)S(1)} %get-tuple-element.6), channel_id=1, source_target_pairs={{0,32},{32,64},{64,96},{96,128},{128,160},{160,192},{192,224},{224... | collective-permute-start | bytes 196616 | tf_op jit(solution)/shard_map/ppermute | solution.py:103
  12.2 7.7 %collective-permute-start.1 = (bf16[8,4,2,512]{3,1,2,0:T(4,128)(2,1)S(1)}, bf16[8,4,2,512]{3,1,2,0:T(4,128)(2,1)S(1)}, u32[]{:S(2)}, u32[]{:S(2)}) collective-permute-start(bf16[8,4,2,512]{3,1,2,0:T(4,128)(2,1)S(1)} %get-tuple-element.6), channel_id=1, source_target_pairs={{0,480},{32,0},{64,32},{96,64},{128,96},{160,128},{192,160},{224,1... | collective-permute-start | bytes 196616 | tf_op jit(solution)/shard_map/ppermute | solution.py:106
  14.6 7.3 %collective-permute-start.2 = (bf16[8,4,2,512]{3,1,2,0:T(4,128)(2,1)S(1)}, bf16[8,4,2,512]{3,1,2,0:T(4,128)(2,1)S(1)}, u32[]{:S(2)}, u32[]{:S(2)}) collective-permute-start(bf16[8,4,2,512]{3,1,2,0:T(4,128)(2,1)S(1)} %collective-permute-done), channel_id=1, source_target_pairs={{0,32},{32,64},{64,96},{96,128},{128,160},{160,192},{192,224},{224... | collective-permute-start | bytes 196616 | tf_op jit(solution)/shard_map/ppermute | solution.py:103
  19.9 7.5 %collective-permute-start.3 = (bf16[8,4,2,512]{3,1,2,0:T(4,128)(2,1)S(1)}, bf16[8,4,2,512]{3,1,2,0:T(4,128)(2,1)S(1)}, u32[]{:S(2)}, u32[]{:S(2)}) collective-permute-start(bf16[8,4,2,512]{3,1,2,0:T(4,128)(2,1)S(1)} %collective-permute-done.1), channel_id=1, source_target_pairs={{0,480},{32,0},{64,32},{96,64},{128,96},{160,128},{192,160},{224,1... | collective-permute-start | bytes 196616 | tf_op jit(solution)/shard_map/ppermute | solution.py:106
  21.9 7.5 %collective-permute-start.4 = (bf16[8,4,2,512]{3,1,2,0:T(4,128)(2,1)S(1)}, bf16[8,4,2,512]{3,1,2,0:T(4,128)(2,1)S(1)}, u32[]{:S(2)}, u32[]{:S(2)}) collective-permute-start(bf16[8,4,2,512]{3,1,2,0:T(4,128)(2,1)S(1)} %collective-permute-done.2), channel_id=1, source_target_pairs={{0,32},{32,64},{64,96},{96,128},{128,160},{160,192},{192,224},{224... | collective-permute-start | bytes 196616 | tf_op jit(solution)/shard_map/ppermute | solution.py:103
  27.4 7.5 %collective-permute-start.5 = (bf16[8,4,2,512]{3,1,2,0:T(4,128)(2,1)S(1)}, bf16[8,4,2,512]{3,1,2,0:T(4,128)(2,1)S(1)}, u32[]{:S(2)}, u32[]{:S(2)}) collective-permute-start(bf16[8,4,2,512]{3,1,2,0:T(4,128)(2,1)S(1)} %collective-permute-done.3), channel_id=1, source_target_pairs={{0,480},{32,0},{64,32},{96,64},{128,96},{160,128},{192,160},{224,1... | collective-permute-start | bytes 196616 | tf_op jit(solution)/shard_map/ppermute | solution.py:106
  29.5 7.5 %collective-permute-start.6 = (bf16[8,4,2,512]{3,1,2,0:T(4,128)(2,1)S(1)}, bf16[8,4,2,512]{3,1,2,0:T(4,128)(2,1)S(1)}, u32[]{:S(2)}, u32[]{:S(2)}) collective-permute-start(bf16[8,4,2,512]{3,1,2,0:T(4,128)(2,1)S(1)} %collective-permute-done.4), channel_id=1, source_target_pairs={{0,32},{32,64},{64,96},{96,128},{128,160},{160,192},{192,224},{224... | collective-permute-start | bytes 196616 | tf_op jit(solution)/shard_map/ppermute | solution.py:103
  35.0 7.5 %collective-permute-start.7 = (bf16[8,4,2,512]{3,1,2,0:T(4,128)(2,1)S(1)}, bf16[8,4,2,512]{3,1,2,0:T(4,128)(2,1)S(1)}, u32[]{:S(2)}, u32[]{:S(2)}) collective-permute-start(bf16[8,4,2,512]{3,1,2,0:T(4,128)(2,1)S(1)} %collective-permute-done.5), channel_id=1, source_target_pairs={{0,480},{32,0},{64,32},{96,64},{128,96},{160,128},{192,160},{224,1... | collective-permute-start | bytes 196616 | tf_op jit(solution)/shard_map/ppermute | solution.py:106
  37.0 7.5 %collective-permute-start.8 = (bf16[8,4,2,512]{3,1,2,0:T(4,128)(2,1)S(1)}, bf16[8,4,2,512]{3,1,2,0:T(4,128)(2,1)S(1)}, u32[]{:S(2)}, u32[]{:S(2)}) collective-permute-start(bf16[8,4,2,512]{3,1,2,0:T(4,128)(2,1)S(1)} %collective-permute-done.6), channel_id=1, source_target_pairs={{0,32},{32,64},{64,96},{96,128},{128,160},{160,192},{192,224},{224... | collective-permute-start | bytes 196616 | tf_op jit(solution)/shard_map/ppermute | solution.py:103
  42.5 7.5 %collective-permute-start.9 = (bf16[8,4,2,512]{3,1,2,0:T(4,128)(2,1)S(1)}, bf16[8,4,2,512]{3,1,2,0:T(4,128)(2,1)S(1)}, u32[]{:S(2)}, u32[]{:S(2)}) collective-permute-start(bf16[8,4,2,512]{3,1,2,0:T(4,128)(2,1)S(1)} %collective-permute-done.7), channel_id=1, source_target_pairs={{0,480},{32,0},{64,32},{96,64},{128,96},{160,128},{192,160},{224,1... | collective-permute-start | bytes 196616 | tf_op jit(solution)/shard_map/ppermute | solution.py:106
  44.6 7.5 %collective-permute-start.10 = (bf16[8,4,2,512]{3,1,2,0:T(4,128)(2,1)S(1)}, bf16[8,4,2,512]{3,1,2,0:T(4,128)(2,1)S(1)}, u32[]{:S(2)}, u32[]{:S(2)}) collective-permute-start(bf16[8,4,2,512]{3,1,2,0:T(4,128)(2,1)S(1)} %collective-permute-done.8), channel_id=1, source_target_pairs={{0,32},{32,64},{64,96},{96,128},{128,160},{160,192},{192,224},{224... | collective-permute-start | bytes 196616 | tf_op jit(solution)/shard_map/ppermute | solution.py:103
  50.1 7.5 %collective-permute-start.11 = (bf16[8,4,2,512]{3,1,2,0:T(4,128)(2,1)S(1)}, bf16[8,4,2,512]{3,1,2,0:T(4,128)(2,1)S(1)}, u32[]{:S(2)}, u32[]{:S(2)}) collective-permute-start(bf16[8,4,2,512]{3,1,2,0:T(4,128)(2,1)S(1)} %collective-permute-done.9), channel_id=1, source_target_pairs={{0,480},{32,0},{64,32},{96,64},{128,96},{160,128},{192,160},{224,1... | collective-permute-start | bytes 196616 | tf_op jit(solution)/shard_map/ppermute | solution.py:106
  52.1 7.5 %collective-permute-start.12 = (bf16[8,4,2,512]{3,1,2,0:T(4,128)(2,1)S(1)}, bf16[8,4,2,512]{3,1,2,0:T(4,128)(2,1)S(1)}, u32[]{:S(2)}, u32[]{:S(2)}) collective-permute-start(bf16[8,4,2,512]{3,1,2,0:T(4,128)(2,1)S(1)} %collective-permute-done.10), channel_id=1, source_target_pairs={{0,32},{32,64},{64,96},{96,128},{128,160},{160,192},{192,224},{224... | collective-permute-start | bytes 196616 | tf_op jit(solution)/shard_map/ppermute | solution.py:103
  57.6 7.6 %collective-permute-start.13 = (bf16[8,4,2,512]{3,1,2,0:T(4,128)(2,1)S(1)}, bf16[8,4,2,512]{3,1,2,0:T(4,128)(2,1)S(1)}, u32[]{:S(2)}, u32[]{:S(2)}) collective-permute-start(bf16[8,4,2,512]{3,1,2,0:T(4,128)(2,1)S(1)} %collective-permute-done.11), channel_id=1, source_target_pairs={{0,480},{32,0},{64,32},{96,64},{128,96},{160,128},{192,160},{224,1... | collective-permute-start | bytes 196616 | tf_op jit(solution)/shard_map/ppermute | solution.py:106
  59.7 6.8 %collective-permute-start.14 = (bf16[8,4,2,512]{3,1,2,0:T(4,128)(2,1)S(1)}, bf16[8,4,2,512]{3,1,2,0:T(4,128)(2,1)S(1)}, u32[]{:S(2)}, u32[]{:S(2)}) collective-permute-start(bf16[8,4,2,512]{3,1,2,0:T(4,128)(2,1)S(1)} %collective-permute-done.12), channel_id=1, source_target_pairs={{0,32},{32,64},{64,96},{96,128},{128,160},{160,192},{192,224},{224... | collective-permute-start | bytes 196616 | tf_op jit(solution)/shard_map/ppermute | solution.py:103
  66.6 18.3 %collective-permute-start.15 = (bf16[8,64,1,512]{3,1,2,0:T(8,128)(2,1)S(1)}, bf16[8,64,1,512]{3,1,2,0:T(8,128)(2,1)S(1)}, u32[]{:S(2)}, u32[]{:S(2)}) collective-permute-start(bf16[8,64,1,512]{3,1,2,0:T(8,128)(2,1)S(1)} %get-tuple-element.10), channel_id=1, source_target_pairs={{0,1},{1,2},{2,3},{3,4},{4,5},{5,6},{6,7},{7,8},{8,9},{9,10},{10,1... | collective-permute-start | bytes 1572872 | tf_op jit(solution)/shard_map/ppermute | solution.py:14
  77.6 12.8 %collective-permute-start.16 = (bf16[8,64,1,512]{3,1,2,0:T(8,128)(2,1)S(1)}, bf16[8,64,1,512]{3,1,2,0:T(8,128)(2,1)S(1)}, u32[]{:S(2)}, u32[]{:S(2)}) collective-permute-start(bf16[8,64,1,512]{3,1,2,0:T(8,128)(2,1)S(1)} %get-tuple-element.11), channel_id=1, source_target_pairs={{1,0},{2,1},{3,2},{4,3},{5,4},{6,5},{7,6},{8,7},{9,8},{10,9},{11,1... | collective-permute-start | bytes 1572872 | tf_op jit(solution)/shard_map/ppermute | solution.py:15
  98.2 20.2 %copy-start.4 = (bf16[8,4,2,512]{3,2,1,0:T(2,128)(2,1)S(1)}, bf16[8,4,2,512]{3,2,1,0:T(2,128)(2,1)}, u32[]{:S(2)}) copy-start(bf16[8,4,2,512]{3,2,1,0:T(2,128)(2,1)} %param.6) | copy-start | bytes 196612
  119.2 5.8 %collective-permute-start.17 = (bf16[8,1,4,256]{3,2,1,0:T(4,128)(2,1)S(1)}, bf16[8,1,4,256]{3,2,1,0:T(4,128)(2,1)S(1)}, u32[]{:S(2)}, u32[]{:S(2)}) collective-permute-start(bf16[8,1,4,256]{3,2,1,0:T(4,128)(2,1)S(1)} %get-tuple-element.25), channel_id=1, source_target_pairs={{0,32},{32,64},{64,96},{96,128},{128,160},{160,192},{192,224},{224... | collective-permute-start | bytes 49160 | tf_op jit(solution)/shard_map/ppermute | solution.py:14
  122.9 6.6 %collective-permute-start.18 = (bf16[8,1,4,256]{3,2,1,0:T(4,128)(2,1)S(1)}, bf16[8,1,4,256]{3,2,1,0:T(4,128)(2,1)S(1)}, u32[]{:S(2)}, u32[]{:S(2)}) collective-permute-start(bf16[8,1,4,256]{3,2,1,0:T(4,128)(2,1)S(1)} %get-tuple-element.24), channel_id=1, source_target_pairs={{32,0},{64,32},{96,64},{128,96},{160,128},{192,160},{224,192},{256... | collective-permute-start | bytes 49160 | tf_op jit(solution)/shard_map/ppermute | solution.py:15
  129.6 6.8 %collective-permute-start.19 = (bf16[8,10,1,256]{3,2,1,0:T(2,128)(2,1)S(1)}, bf16[8,10,1,256]{3,2,1,0:T(2,128)(2,1)S(1)}, u32[]{:S(2)}, u32[]{:S(2)}) collective-permute-start(bf16[8,10,1,256]{3,2,1,0:T(2,128)(2,1)S(1)} %get-tuple-element.22), channel_id=1, source_target_pairs={{0,1},{1,2},{2,3},{3,4},{4,5},{5,6},{6,7},{7,8},{8,9},{9,10},{10,1... | collective-permute-start | bytes 122888 | tf_op jit(solution)/shard_map/ppermute | solution.py:14
  134.1 7.0 %collective-permute-start.20 = (bf16[8,10,1,256]{3,2,1,0:T(2,128)(2,1)S(1)}, bf16[8,10,1,256]{3,2,1,0:T(2,128)(2,1)S(1)}, u32[]{:S(2)}, u32[]{:S(2)}) collective-permute-start(bf16[8,10,1,256]{3,2,1,0:T(2,128)(2,1)S(1)} %get-tuple-element.23), channel_id=1, source_target_pairs={{1,0},{2,1},{3,2},{4,3},{5,4},{6,5},{7,6},{8,7},{9,8},{10,9},{11,1... | collective-permute-start | bytes 122888 | tf_op jit(solution)/shard_map/ppermute | solution.py:15
  156.3 2.4 %copy-start.1 = (bf16[1,3,3,256,256]{4,3,2,1,0:T(8,128)(2,1)S(1)}, bf16[1,3,3,256,256]{4,3,2,1,0:T(8,128)(2,1)}, u32[]{:S(2)}) copy-start(bf16[1,3,3,256,256]{4,3,2,1,0:T(8,128)(2,1)} %copy.79) | copy-start | bytes 3538948
  160.8 2.1 %copy-start.5 = (bf16[256,128]{1,0:T(8,128)(2,1)S(1)}, bf16[256,128]{1,0:T(8,128)(2,1)}, u32[]{:S(2)}) copy-start(bf16[256,128]{1,0:T(8,128)(2,1)} %param.11) | copy-start | bytes 196612
  160.8 16.4 %copy-start.3 = (bf16[3,3,3,128,128]{4,3,2,1,0:T(8,128)(2,1)S(1)}, bf16[3,3,3,128,128]{4,3,2,1,0:T(8,128)(2,1)}, u32[]{:S(2)}) copy-start(bf16[3,3,3,128,128]{4,3,2,1,0:T(8,128)(2,1)} %param.9) | copy-start | bytes 2654212
  163.6 5.3 %collective-permute-start.21 = (bf16[8,1,8,128]{3,2,1,0:T(8,128)(2,1)S(1)}, bf16[8,1,8,128]{3,2,1,0:T(8,128)(2,1)S(1)}, u32[]{:S(2)}, u32[]{:S(2)}) collective-permute-start(bf16[8,1,8,128]{3,2,1,0:T(8,128)(2,1)S(1)} %get-tuple-element.20), channel_id=1, source_target_pairs={{0,32},{32,64},{64,96},{96,128},{128,160},{160,192},{192,224},{224... | collective-permute-start | bytes 49160 | tf_op jit(solution)/shard_map/ppermute | solution.py:14
  165.5 6.6 %collective-permute-start.22 = (bf16[8,1,8,128]{3,2,1,0:T(8,128)(2,1)S(1)}, bf16[8,1,8,128]{3,2,1,0:T(8,128)(2,1)S(1)}, u32[]{:S(2)}, u32[]{:S(2)}) collective-permute-start(bf16[8,1,8,128]{3,2,1,0:T(8,128)(2,1)S(1)} %get-tuple-element.21), channel_id=1, source_target_pairs={{32,0},{64,32},{96,64},{128,96},{160,128},{192,160},{224,192},{256... | collective-permute-start | bytes 49160 | tf_op jit(solution)/shard_map/ppermute | solution.py:15
  172.2 5.1 %collective-permute-start.23 = (bf16[8,18,1,128]{3,2,1,0:T(2,128)(2,1)S(1)}, bf16[8,18,1,128]{3,2,1,0:T(2,128)(2,1)S(1)}, u32[]{:S(2)}, u32[]{:S(2)}) collective-permute-start(bf16[8,18,1,128]{3,2,1,0:T(2,128)(2,1)S(1)} %get-tuple-element.18), channel_id=1, source_target_pairs={{0,1},{1,2},{2,3},{3,4},{4,5},{5,6},{6,7},{7,8},{8,9},{9,10},{10,1... | collective-permute-start | bytes 110600 | tf_op jit(solution)/shard_map/ppermute | solution.py:14
  175.2 6.9 %collective-permute-start.24 = (bf16[8,18,1,128]{3,2,1,0:T(2,128)(2,1)S(1)}, bf16[8,18,1,128]{3,2,1,0:T(2,128)(2,1)S(1)}, u32[]{:S(2)}, u32[]{:S(2)}) collective-permute-start(bf16[8,18,1,128]{3,2,1,0:T(2,128)(2,1)S(1)} %get-tuple-element.19), channel_id=1, source_target_pairs={{1,0},{2,1},{3,2},{4,3},{5,4},{6,5},{7,6},{8,7},{9,8},{10,9},{11,1... | collective-permute-start | bytes 110600 | tf_op jit(solution)/shard_map/ppermute | solution.py:15
Sparse Core Ops, SparseCore 0:
  14.5 82.7 all-gather.1
